TPU v7x, 32 devices: a whole 2x2x4 slice. The times are simulated.
32 devices in a mesh: groups: 2 (over y), row: 4 (over x, core), col: 4 (over z).
Axes of the slice: x: 2, y: 2, z: 4, core: 2. Of those that a mesh axis runs over, the one named last changes fastest.
Arguments:
- features: float32 [32, 65536], P(None, ('groups', 'row', 'col')), parts along dimension 1, may hold values from -6 to 6
- noise: float32 [65536], P(('groups', 'row', 'col')), parts along dimension 0, may hold values from 0.5 to 4
- solution: float32 [16, 65536], P(None, ('groups', 'row', 'col')), parts along dimension 1, may hold values from -6 to 6
- residual: float32 [16, 65536], P(None, ('groups', 'row', 'col')), parts along dimension 1, may hold values from -12 to 12
- direction: float32 [16, 65536], P(None, ('groups', 'row', 'col')), parts along dimension 1, may hold values from -12 to 12
- tile_rows: int32 [8, 4, 64], P(('groups', 'row'), 'col'), parts along dimension 0, may hold values from 0 to 15, as said below
- tile_cols: int32 [8, 4, 64], P(('groups', 'row'), 'col'), parts along dimension 0, may hold values from 0 to 15, as said below
- tile_count: int32 [8, 4], P(('groups', 'row'), 'col'), parts along dimension 0, may hold values from 1 to 64, as said below
Outputs:
- solution_next: float32 [16, 65536], P(None, ('groups', 'row', 'col')), parts along dimension 1
- residual_next: float32 [16, 65536], P(None, ('groups', 'row', 'col')), parts along dimension 1
- direction_next: float32 [16, 65536], P(None, ('groups', 'row', 'col')), parts along dimension 1
There are 2 independent parts, one for each index of `groups`. A program takes and returns all parts, laid end to end along the dimension named above; each array names one. Nothing has to cross between parts.
Inputs may be any that keep to these rules, and one draw needn't show every extreme that they name: `tile_rows`: every listed slot names a tile with I <= J; the slots of one device name distinct tiles. `tile_cols`: see tile_rows. `tile_count`: some device of every problem lists 64 tiles.
All inputs are finite; a program needn't handle non-finite values.
Results may differ from a plain program's by a relative error of at most 0.0003.
Values sent between devices are 32-bit elements; how exact they have to be, the bound alone decides.
A program may use at most 64 MiB of HBM per device.

v0:
```python
import math
import jax
import jax.numpy as jnp
from jax import lax
from jax.sharding import PartitionSpec as P

BLK_DEV = 4
HIGH = lax.Precision.HIGHEST


def tile_kernel(row_points, col_points):
    inner = lax.dot_general(
        row_points,
        col_points,
        (((0,), (0,)), ((), ())),
        precision=HIGH,
        preferred_element_type=jnp.float32,
    )
    row_norms = jnp.sum(row_points * row_points, 0)
    col_norms = jnp.sum(col_points * col_points, 0)
    dist_sq = jnp.maximum(row_norms[:, None] + col_norms[None, :] - 2.0 * inner, 0.0)
    radius = jnp.sqrt(dist_sq) / (1.5 * math.sqrt(row_points.shape[0]))
    inside = jnp.maximum(1.0 - radius, 0.0)
    return inside**4 * (4.0 * radius + 1.0)


def gram(left, right):
    return lax.dot_general(
        left, right, (((1,), (1,)), ((), ())), precision=HIGH, preferred_element_type=jnp.float32
    )


def symmetric(matrix):
    return 0.5 * (matrix + matrix.T)


def spd_solve(matrix, target):
    lower = jnp.linalg.cholesky(matrix)
    half_way = lax.linalg.triangular_solve(lower, target, left_side=True, lower=True)
    return lax.linalg.triangular_solve(
        lower, half_way, left_side=True, lower=True, transpose_a=True
    )


def apply_left(coeffs, field):
    return lax.dot_general(
        coeffs, field, (((0,), (0,)), ((), ())), precision=HIGH, preferred_element_type=jnp.float32
    )


def add_at(running, addend, start):
    axis_last = running.ndim - 1
    current = lax.dynamic_slice_in_dim(running, start, addend.shape[-1], axis_last)
    return lax.dynamic_update_slice_in_dim(running, current + addend, start, axis_last)


def reduce_rows(row_image, row_degree):
    return (
        lax.psum_scatter(row_image, "col", scatter_dimension=1, tiled=True),
        lax.psum_scatter(row_degree, "col", scatter_dimension=0, tiled=True),
    )


def reduce_cols(col_image, col_degree):
    return (
        lax.psum_scatter(col_image, "row", scatter_dimension=1, tiled=True),
        lax.psum_scatter(col_degree, "row", scatter_dimension=0, tiled=True),
    )


def on_device(features, noise, solution, residual, direction, tile_rows, tile_cols, tile_count):
    block_width = features.shape[1] // BLK_DEV
    row_slots = tile_rows[0, 0]
    col_slots = tile_cols[0, 0]
    tile_total = tile_count[0, 0]
    rank_row = lax.axis_index("row")
    rank_col = lax.axis_index("col")
    span = lax.axis_size("col") * BLK_DEV
    row_feat, row_dir = (
        lax.all_gather(features, "col", axis=1, tiled=True),
        lax.all_gather(direction, "col", axis=1, tiled=True),
    )
    col_feat, col_dir = (
        lax.all_gather(features, "row", axis=1, tiled=True),
        lax.all_gather(direction, "row", axis=1, tiled=True),
    )
    side_count = direction.shape[0]
    initial = (
        jnp.zeros((side_count, row_feat.shape[1]), jnp.float32),
        jnp.zeros((row_feat.shape[1],), jnp.float32),
        jnp.zeros((side_count, col_feat.shape[1]), jnp.float32),
        jnp.zeros((col_feat.shape[1],), jnp.float32),
    )

    def one_tile(tile_slot, carried):
        to_row, deg_row, to_col, deg_col = carried
        local_i = row_slots[tile_slot]
        local_j = col_slots[tile_slot]
        start_i = local_i * block_width
        start_j = local_j * block_width
        used_flag = (tile_slot < tile_total).astype(jnp.float32)
        kernel = (
            tile_kernel(
                lax.dynamic_slice_in_dim(row_feat, start_i, block_width, 1),
                lax.dynamic_slice_in_dim(col_feat, start_j, block_width, 1),
            )
            * used_flag
        )
        dir_cols = lax.dynamic_slice_in_dim(col_dir, start_j, block_width, 1)
        row_term = lax.dot_general(
            dir_cols,
            kernel,
            (((1,), (1,)), ((), ())),
            precision=HIGH,
            preferred_element_type=jnp.float32,
        )
        to_row = add_at(to_row, row_term, start_i)
        deg_row = add_at(deg_row, jnp.sum(kernel, 1), start_i)
        big_i = rank_row * span + local_i
        big_j = local_j // BLK_DEV * span + rank_col * BLK_DEV + local_j % BLK_DEV
        mirror = (big_i != big_j).astype(jnp.float32)
        dir_rows = lax.dynamic_slice_in_dim(row_dir, start_i, block_width, 1)
        col_term = (
            lax.dot_general(
                dir_rows,
                kernel,
                (((1,), (0,)), ((), ())),
                precision=HIGH,
                preferred_element_type=jnp.float32,
            )
            * mirror
        )
        to_col = add_at(to_col, col_term, start_j)
        deg_col = add_at(deg_col, jnp.sum(kernel, 0) * mirror, start_j)
        return (to_row, deg_row, to_col, deg_col)

    def one_turn(turn_index, carried):
        for inner_step in range(4):
            carried = one_tile(turn_index * 4 + inner_step, carried)
        return carried

    carried = lax.fori_loop(0, row_slots.shape[0] // 4, one_turn, initial)
    row_image, row_degree = reduce_rows(carried[0], carried[1])
    col_image, col_degree = reduce_cols(carried[2], carried[3])
    degree = row_degree + col_degree
    image = (noise + degree)[None, :] * direction + row_image + col_image
    curv_sum, norm_sum = lax.psum(
        (gram(direction, image), gram(residual, residual)), ("row", "col")
    )
    curvature = symmetric(curv_sum)
    norms_now = symmetric(norm_sum)
    alpha = spd_solve(curvature, norms_now)
    residual_next = residual - apply_left(alpha, image)
    norms_next = symmetric(lax.psum(gram(residual_next, residual_next), ("row", "col")))
    solution_next = solution + apply_left(alpha, direction)
    beta = spd_solve(norms_now, norms_next)
    direction_next = residual_next + apply_left(beta, direction)
    return (solution_next, residual_next, direction_next)


def solution(mesh):
    in_specs = (
        P(None, ("groups", "row", "col")),
        P(("groups", "row", "col")),
        P(None, ("groups", "row", "col")),
        P(None, ("groups", "row", "col")),
        P(None, ("groups", "row", "col")),
        P(("groups", "row"), "col", None),
        P(("groups", "row"), "col", None),
        P(("groups", "row"), "col"),
    )
    out_specs = (
        P(None, ("groups", "row", "col")),
        P(None, ("groups", "row", "col")),
        P(None, ("groups", "row", "col")),
    )
    return jax.shard_map(
        on_device, mesh=mesh, in_specs=in_specs, out_specs=out_specs, check_vma=False
    )
```

profile of v0, /device:TPU:0, one launch (start us, length us, event | category | flops | bytes accessed | tf_op | source)
XLA Modules:
  0.0 874.8 jit_solution(3112990234694962577)
XLA Ops:
  8.8 20.4 %all_gather.15 = f32[16,8192]{1,0:T(8,128)S(1)} all-gather(f32[16,2048]{1,0:T(8,128)S(1)} %copy-done), channel_id=1, replica_groups=mesh['groups'=2,'row'=4,'col'=4] {'col'}, dimensions={1}, use_global_device_ids=true | all-gather | bytes 655360 | tf_op jit(solution)/shard_map/all_gather | solution.py:81
  29.2 7.2 all_gather.12
  36.4 6.0 all-gather.3.cloned.1.call-done
  42.4 17.7 %all-gather.5.cloned.1.call-done = f32[32,8192]{1,0:T(8,128)} async-done(((f32[32,2048]{1,0:T(8,128)}), f32[32,8192]{1,0:T(8,128)}) %all-gather.5.cloned.1.call-update) | async-done | bytes 1048592 | tf_op jit(solution)/shard_map/all_gather | solution.py:84
  60.9 658.1 %while.22 = (s32[]{:T(128)}, f32[16,8192]{1,0:T(8,128)S(1)}, f32[8192]{0:T(1024)S(1)}, f32[16,8192]{1,0:T(8,128)S(1)}, f32[8192]{0:T(1024)S(1)}, /*index=5*/s32[...) while((s32[]{:T(128)}, f32[16,8192]{1,0:T(8,128)S(1)}, ...), condition=%wide.region_17.18_spmd, body=%wide.region_0.17_spmd.sunk | while | flops 821393472 | bytes 14518369 | solution.py:142
  83.6 2.7 fusion.148
  88.2 2.7 fusion.150
  92.8 2.7 fusion.152
  124.8 2.7 fusion.148
  129.4 2.7 fusion.150
  134.0 2.7 fusion.152
  165.9 2.7 fusion.148
  170.5 2.7 fusion.150
  175.1 2.7 fusion.152
  207.0 2.7 fusion.148
  211.6 2.7 fusion.150
  216.2 2.7 fusion.152
  248.2 2.7 fusion.148
  252.8 2.7 fusion.150
  261.9 2.6 fusion.154
  289.3 2.7 fusion.148
  293.9 2.7 fusion.150
  298.5 2.7 fusion.152
  330.4 2.7 fusion.148
  335.0 2.7 fusion.150
  339.6 2.7 fusion.152
  344.2 2.6 fusion.154
  371.5 2.7 fusion.148
  376.2 2.7 fusion.150
  380.7 2.7 fusion.152
  412.7 2.7 fusion.148
  417.3 2.7 fusion.150
  421.9 2.7 fusion.152
  426.5 2.6 fusion.154
  453.8 2.7 fusion.148
  458.4 2.7 fusion.150
  463.0 2.7 fusion.152
  467.6 2.6 fusion.154
  494.9 2.7 fusion.148
  499.5 2.7 fusion.150
  504.1 2.7 fusion.152
  536.1 2.7 fusion.148
  540.7 2.7 fusion.150
  545.3 2.7 fusion.152
  577.2 2.7 fusion.148
  581.8 2.7 fusion.150
  586.4 2.6 fusion.152
  590.9 2.6 fusion.154
  618.3 2.7 fusion.148
  622.9 2.7 fusion.150
  627.5 2.7 fusion.152
  632.1 2.6 fusion.154
  659.4 2.7 fusion.148
  664.0 2.7 fusion.150
  673.2 2.6 fusion.154
  700.5 2.7 fusion.148
  705.1 2.7 fusion.150
  709.7 2.7 fusion.152
  714.3 2.7 fusion.154
  723.8 10.9 %all-reduce.1 = f32[8192]{0:T(1024)S(1)} all-reduce(f32[8192]{0:T(1024)S(1)} %get-tuple-element.410), channel_id=3, replica_groups=mesh['groups'=2,'row'=4,'col'=4] {'row'}, use_global_device_ids=true, to_apply=%region_19.20.clone | all-reduce | flops 8192 | bytes 65536
  734.7 19.5 %all-reduce = f32[8192]{0:T(1024)S(1)} all-reduce(f32[8192]{0:T(1024)S(1)} %get-tuple-element.409), channel_id=2, replica_groups=mesh['groups'=2,'row'=4,'col'=4] {'col'}, use_global_device_ids=true, to_apply=%region_18.19.clone | all-reduce | flops 8192 | bytes 65536
  754.3 9.7 %reduce-scatter.5.cloned.1.call-done = f32[16,2048]{1,0:T(8,128)} async-done(((f32[16,8192]{1,0:T(8,128)}), f32[16,2048]{1,0:T(8,128)}) %reduce-scatter.5.cloned.1.call-update) | async-done | bytes 131088 | tf_op jit(solution)/shard_map/reduce_scatter | solution.py:66
  765.3 60.8 %all-reduce.2 = (f32[16,16]{1,0:T(8,128)S(1)}, f32[16,16]{1,0:T(8,128)S(1)}) all-reduce(f32[16,16]{1,0:T(8,128)S(1)} %fusion.77, f32[16,16]{1,0:T(8,128)S(1)} %convolution_bitcast_fusion), channel_id=1, replica_groups=mesh['groups'=2,'row'=4,'col'=4] {'row','col'}, use_global_device_ids=true, to_apply=%region_25.27 | all-reduce | flops 512 | bytes 4096 | tf_op jit(solution)/shard_map/psum | solution.py:147
  831.3 30.5 %psum.23 = f32[16,16]{1,0:T(8,128)S(1)} all-reduce(f32[16,16]{1,0:T(8,128)S(1)} %fusion.78), channel_id=1, replica_groups=mesh['groups'=2,'row'=4,'col'=4] {'row','col'}, use_global_device_ids=true, to_apply=%region_26.30 | all-reduce | flops 256 | bytes 2048 | tf_op jit(solution)/shard_map/psum | solution.py:154
  (386 shorter events, 207.0 us)
Async XLA Ops:
  7.2 35.2 %all-gather.3.cloned.1.call-start = ((), (), s32[]{:S(2)}) async-start(), calls=%async_computation.2 | async-start | bytes 1310720 | tf_op jit(solution)/shard_map/all_gather | solution.py:80
  7.9 0.9 copy-start
  7.9 52.2 %all-gather.5.cloned.1.call-start = ((), (), s32[]{:S(2)}) async-start(), calls=%async_computation.3 | async-start | bytes 1310720 | tf_op jit(solution)/shard_map/all_gather | solution.py:84
  8.7 745.7 %reduce-scatter.3.cloned.1.call-start = ((), (), s32[]{:S(2)}) async-start(), calls=%async_computation.4 | async-start | bytes 655360 | tf_op jit(solution)/shard_map/reduce_scatter | solution.py:59
  42.4 17.9 %copy-start.4 = (f32[32,8192]{1,0:T(8,128)S(1)}, f32[32,8192]{1,0:T(8,128)}, u32[]{:S(2)}) copy-start(f32[32,8192]{1,0:T(8,128)} %all-gather.3.cloned.1.call-done) | copy-start | bytes 3145732
  60.2 0.7 copy-start.8
  60.2 0.7 copy-start.9
  719.0 0.8 copy-start.2
  719.0 1.0 copy-start.1
  719.8 44.2 %reduce-scatter.5.cloned.1.call-start = ((), (), s32[]{:S(2)}) async-start(), calls=%async_computation.5 | async-start | bytes 655360 | tf_op jit(solution)/shard_map/reduce_scatter | solution.py:66
  719.9 3.7 copy-start.5
  720.4 0.7 copy-start.13
  721.1 0.7 copy-start.12
  734.7 19.6 %copy-start.11 = (f32[2048]{0:T(1024)S(1)}, f32[2048]{0:T(1024)}, u32[]{:S(2)}) copy-start(f32[2048]{0:T(1024)} %param.16) | copy-start | bytes 24580
  764.0 66.7 %copy-start.7 = (f32[16,2048]{1,0:T(8,128)S(1)}, f32[16,2048]{1,0:T(8,128)}, u32[]{:S(2)}) copy-start(f32[16,2048]{1,0:T(8,128)} %reduce-scatter.5.cloned.1.call-done) | copy-start | bytes 393220
  765.3 65.5 %copy-start.6 = (f32[16,2048]{1,0:T(8,128)S(1)}, f32[16,2048]{1,0:T(8,128)}, u32[]{:S(2)}) copy-start(f32[16,2048]{1,0:T(8,128)} %reduce-scatter.3.cloned.1.call-done) | copy-start | bytes 393220
  831.1 35.2 %copy-start.3 = (f32[16,2048]{1,0:T(8,128)}, f32[16,2048]{1,0:T(8,128)S(1)}, u32[]{:S(2)}) copy-start(f32[16,2048]{1,0:T(8,128)S(1)} %convolution_subtract_fusion) | copy-start | bytes 393220
  866.3 1.0 copy-start.10
Sparse Core Ops, SparseCore 0:
  9.6 32.7 all-gather.2
  44.0 16.1 all-gather.4
  719.9 21.7 reduce-scatter.2
  744.1 19.8 reduce-scatter.4
where the time goes:
time: 883 us; the launch traced here: 875 us
  loops' own time  326 us (37%)
  matrix products  276 us (31%)
  blocking collectives  149 us (17%)
  other arithmetic  46.4 us (5%)
  waiting for transfers between devices  35.3 us (4%)
  local copies, waits for them, and re-layouts  25.9 us (3%)
  between operations  15.3 us (2%)
    another operation x1, loops' own time, on_device(): carried = lax.fori_loop(0, row_slots.shape[0] // 4, one_turn, initial)  326 us
    dot_general x64, matrix products, tile_kernel(): lax.dot_general(row_points, col_points, (((0,), (0,)), ((), ())), precisi...  170 us
    dot_general x64, matrix products, one_tile(): lax.dot_general(dir_cols, kernel, (((1,), (1,)), ((), ())), precision=HIG...  61.8 us
    psum x1, blocking collectives, on_device(): lax.psum((gram(direction, image), gram(residual, residual)), ('row', 'col'))  60.8 us
    dot_general x64, matrix products, one_tile(): lax.dot_general(dir_rows, kernel, (((1,), (0,)), ((), ())), precision=HIG...  39.9 us
    psum x1, blocking collectives, on_device(): lax.psum(gram(residual_next, residual_next), ('row', 'col'))  30.5 us
    unnamed x2, blocking collectives  30.4 us
    dynamic_update_slice x128, other arithmetic, add_at(): lax.dynamic_update_slice_in_dim(running, current + addend, start, axis_last)  21.8 us
  transfers between devices with their start and end apart: 4, of which 3 were waited for; matrix products, arithmetic and copies ran while one was open for 0% of the time, Pallas kernels for 0%

commit v1 on v0

--- a/solution.py
+++ b/solution.py
@@ -145,7 +145,7 @@
     degree = row_degree + col_degree
     image = (noise + degree)[None, :] * direction + row_image + col_image
     curv_sum, norm_sum = lax.psum(
-        (gram(direction, image), gram(residual, residual)), ("row", "col")
+        lax.psum((gram(direction, image), gram(residual, residual)), "col"), "row"
     )
     curvature = symmetric(curv_sum)
     norms_now = symmetric(norm_sum)

time: 883 us -> 852 us (0.965)
  blocking collectives: 149 us -> 118 us
    psum x1 -> x2, blocking collectives: 60.8 us -> 29.1 us  [the longest x1 18.9 us: on_device(): lax.psum((gram(direction, image), gram(residual, residual)), 'col')]
where the time goes in v1:
time: 852 us; the launch traced here: 843 us
  loops' own time  326 us (38%)
  matrix products  276 us (32%)
  blocking collectives  118 us (14%)
  other arithmetic  46.4 us (5%)
  waiting for transfers between devices  35.3 us (4%)
  local copies, waits for them, and re-layouts  26 us (3%)
  between operations  15.3 us (2%)
    another operation x1, loops' own time, on_device(): carried = lax.fori_loop(0, row_slots.shape[0] // 4, one_turn, initial)  326 us
    dot_general x64, matrix products, tile_kernel(): lax.dot_general(row_points, col_points, (((0,), (0,)), ((), ())), precisi...  170 us
    dot_general x64, matrix products, one_tile(): lax.dot_general(dir_cols, kernel, (((1,), (1,)), ((), ())), precision=HIG...  61.8 us
    dot_general x64, matrix products, one_tile(): lax.dot_general(dir_rows, kernel, (((1,), (0,)), ((), ())), precision=HIG...  39.9 us
    psum x1, blocking collectives, on_device(): lax.psum(gram(residual_next, residual_next), ('row', 'col'))  30.5 us
    unnamed x2, blocking collectives  30.4 us
    dynamic_update_slice x128, other arithmetic, add_at(): lax.dynamic_update_slice_in_dim(running, current + addend, start, axis_last)  21.8 us
    all_gather x1, blocking collectives, on_device(): lax.all_gather(direction, 'col', axis=1, tiled=True)  20.4 us
  transfers between devices with their start and end apart: 4, of which 3 were waited for; matrix products, arithmetic and copies ran while one was open for 0% of the time, Pallas kernels for 0%

profile of v1, /device:TPU:0, one launch (start us, length us, event | category | flops | bytes accessed | tf_op | source)
XLA Modules:
  0.0 843.0 jit_solution(2346787852783777881)
XLA Ops:
  8.8 20.4 %all_gather.15 = f32[16,8192]{1,0:T(8,128)S(1)} all-gather(f32[16,2048]{1,0:T(8,128)S(1)} %copy-done), channel_id=1, replica_groups=mesh['groups'=2,'row'=4,'col'=4] {'col'}, dimensions={1}, use_global_device_ids=true | all-gather | bytes 655360 | tf_op jit(solution)/shard_map/all_gather | solution.py:81
  29.2 7.2 all_gather.12
  36.4 6.0 all-gather.3.cloned.1.call-done
  42.4 17.7 %all-gather.5.cloned.1.call-done = f32[32,8192]{1,0:T(8,128)} async-done(((f32[32,2048]{1,0:T(8,128)}), f32[32,8192]{1,0:T(8,128)}) %all-gather.5.cloned.1.call-update) | async-done | bytes 1048592 | tf_op jit(solution)/shard_map/all_gather | solution.py:84
  60.9 658.1 %while.22 = (s32[]{:T(128)}, f32[16,8192]{1,0:T(8,128)S(1)}, f32[8192]{0:T(1024)S(1)}, f32[16,8192]{1,0:T(8,128)S(1)}, f32[8192]{0:T(1024)S(1)}, /*index=5*/s32[...) while((s32[]{:T(128)}, f32[16,8192]{1,0:T(8,128)S(1)}, ...), condition=%wide.region_17.18_spmd, body=%wide.region_0.17_spmd.sunk | while | flops 821393472 | bytes 14518369 | solution.py:142
  83.6 2.7 fusion.148
  88.2 2.7 fusion.150
  92.8 2.7 fusion.152
  124.8 2.7 fusion.148
  129.4 2.7 fusion.150
  134.0 2.7 fusion.152
  165.9 2.7 fusion.148
  170.5 2.7 fusion.150
  175.1 2.7 fusion.152
  207.0 2.7 fusion.148
  211.6 2.7 fusion.150
  216.2 2.7 fusion.152
  248.2 2.7 fusion.148
  252.8 2.7 fusion.150
  261.9 2.6 fusion.154
  289.3 2.7 fusion.148
  293.9 2.7 fusion.150
  298.5 2.7 fusion.152
  330.4 2.7 fusion.148
  335.0 2.7 fusion.150
  339.6 2.7 fusion.152
  344.2 2.6 fusion.154
  371.5 2.7 fusion.148
  376.2 2.7 fusion.150
  380.7 2.7 fusion.152
  412.7 2.7 fusion.148
  417.3 2.7 fusion.150
  421.9 2.7 fusion.152
  426.5 2.6 fusion.154
  453.8 2.7 fusion.148
  458.4 2.7 fusion.150
  463.0 2.7 fusion.152
  467.6 2.6 fusion.154
  494.9 2.7 fusion.148
  499.5 2.7 fusion.150
  504.1 2.7 fusion.152
  536.1 2.7 fusion.148
  540.7 2.7 fusion.150
  545.3 2.7 fusion.152
  577.2 2.7 fusion.148
  581.8 2.7 fusion.150
  586.4 2.6 fusion.152
  590.9 2.6 fusion.154
  618.3 2.7 fusion.148
  622.9 2.7 fusion.150
  627.5 2.7 fusion.152
  632.1 2.6 fusion.154
  659.4 2.7 fusion.148
  664.0 2.7 fusion.150
  700.5 2.7 fusion.148
  705.1 2.7 fusion.150
  709.7 2.7 fusion.152
  714.3 2.7 fusion.154
  723.8 10.9 %all-reduce.1 = f32[8192]{0:T(1024)S(1)} all-reduce(f32[8192]{0:T(1024)S(1)} %get-tuple-element.410), channel_id=3, replica_groups=mesh['groups'=2,'row'=4,'col'=4] {'row'}, use_global_device_ids=true, to_apply=%region_19.20.clone | all-reduce | flops 8192 | bytes 65536
  734.7 19.5 %all-reduce = f32[8192]{0:T(1024)S(1)} all-reduce(f32[8192]{0:T(1024)S(1)} %get-tuple-element.409), channel_id=2, replica_groups=mesh['groups'=2,'row'=4,'col'=4] {'col'}, use_global_device_ids=true, to_apply=%region_18.19.clone | all-reduce | flops 8192 | bytes 65536
  754.3 9.7 %reduce-scatter.5.cloned.1.call-done = f32[16,2048]{1,0:T(8,128)} async-done(((f32[16,8192]{1,0:T(8,128)}), f32[16,2048]{1,0:T(8,128)}) %reduce-scatter.5.cloned.1.call-update) | async-done | bytes 131088 | tf_op jit(solution)/shard_map/reduce_scatter | solution.py:66
  765.3 18.9 %all-reduce.2 = (f32[16,16]{1,0:T(8,128)S(1)}, f32[16,16]{1,0:T(8,128)S(1)}) all-reduce(f32[16,16]{1,0:T(8,128)S(1)} %fusion.77, f32[16,16]{1,0:T(8,128)S(1)} %convolution_bitcast_fusion), channel_id=1, replica_groups=mesh['groups'=2,'row'=4,'col'=4] {'col'}, use_global_device_ids=true, to_apply=%region_26.28 | all-reduce | flops 512 | bytes 4096 | tf_op jit(solution)/shard_map/psum | solution.py:148
  784.1 10.3 %all-reduce.3 = (f32[16,16]{1,0:T(8,128)S(1)}, f32[16,16]{1,0:T(8,128)S(1)}) all-reduce(f32[16,16]{1,0:T(8,128)S(1)} %get-tuple-element.457, f32[16,16]{1,0:T(8,128)S(1)} %get-tuple-element.458), channel_id=1, replica_groups=mesh['groups'=2,'row'=4,'col'=4] {'row'}, use_global_device_ids=true, to_apply=%region_27.29 | all-reduce | flops 512 | bytes 4096 | tf_op jit(solution)/shard_map/psum | solution.py:147
  799.6 30.5 %psum.39 = f32[16,16]{1,0:T(8,128)S(1)} all-reduce(f32[16,16]{1,0:T(8,128)S(1)} %fusion.78), channel_id=1, replica_groups=mesh['groups'=2,'row'=4,'col'=4] {'row','col'}, use_global_device_ids=true, to_apply=%region_28.32 | all-reduce | flops 256 | bytes 2048 | tf_op jit(solution)/shard_map/psum | solution.py:154
  (387 shorter events, 209.7 us)
Async XLA Ops:
  7.2 35.2 %all-gather.3.cloned.1.call-start = ((), (), s32[]{:S(2)}) async-start(), calls=%async_computation.2 | async-start | bytes 1310720 | tf_op jit(solution)/shard_map/all_gather | solution.py:80
  7.9 0.9 copy-start
  7.9 52.2 %all-gather.5.cloned.1.call-start = ((), (), s32[]{:S(2)}) async-start(), calls=%async_computation.3 | async-start | bytes 1310720 | tf_op jit(solution)/shard_map/all_gather | solution.py:84
  8.7 745.7 %reduce-scatter.3.cloned.1.call-start = ((), (), s32[]{:S(2)}) async-start(), calls=%async_computation.4 | async-start | bytes 655360 | tf_op jit(solution)/shard_map/reduce_scatter | solution.py:59
  42.4 17.9 %copy-start.4 = (f32[32,8192]{1,0:T(8,128)S(1)}, f32[32,8192]{1,0:T(8,128)}, u32[]{:S(2)}) copy-start(f32[32,8192]{1,0:T(8,128)} %all-gather.3.cloned.1.call-done) | copy-start | bytes 3145732
  60.2 0.7 copy-start.8
  60.2 0.7 copy-start.9
  719.0 0.8 copy-start.2
  719.0 1.0 copy-start.1
  719.8 44.2 %reduce-scatter.5.cloned.1.call-start = ((), (), s32[]{:S(2)}) async-start(), calls=%async_computation.5 | async-start | bytes 655360 | tf_op jit(solution)/shard_map/reduce_scatter | solution.py:66
  719.9 3.7 copy-start.5
  720.4 0.7 copy-start.13
  721.1 0.7 copy-start.12
  734.7 19.6 %copy-start.11 = (f32[2048]{0:T(1024)S(1)}, f32[2048]{0:T(1024)}, u32[]{:S(2)}) copy-start(f32[2048]{0:T(1024)} %param.16) | copy-start | bytes 24580
  765.2 33.8 %copy-start.6 = (f32[16,2048]{1,0:T(8,128)S(1)}, f32[16,2048]{1,0:T(8,128)}, u32[]{:S(2)}) copy-start(f32[16,2048]{1,0:T(8,128)} %reduce-scatter.3.cloned.1.call-done) | copy-start | bytes 393220
  765.2 33.8 %copy-start.7 = (f32[16,2048]{1,0:T(8,128)S(1)}, f32[16,2048]{1,0:T(8,128)}, u32[]{:S(2)}) copy-start(f32[16,2048]{1,0:T(8,128)} %reduce-scatter.5.cloned.1.call-done) | copy-start | bytes 393220
  799.4 35.1 %copy-start.3 = (f32[16,2048]{1,0:T(8,128)}, f32[16,2048]{1,0:T(8,128)S(1)}, u32[]{:S(2)}) copy-start(f32[16,2048]{1,0:T(8,128)S(1)} %convolution_subtract_fusion) | copy-start | bytes 393220
  834.5 1.0 copy-start.10
Sparse Core Ops, SparseCore 0:
  9.6 32.7 all-gather.2
  44.0 16.1 all-gather.4
  719.9 21.7 reduce-scatter.2
  744.1 19.8 reduce-scatter.4
